TPU v7x, 32 devices: a whole 2x2x4 slice. The times are simulated.
32 devices in a mesh: seq: 8 (over z, x), chan: 4 (over y, core).
Axes of the slice: x: 2, y: 2, z: 4, core: 2. Of those that a mesh axis runs over, the one named last changes fastest.
Arguments:
- value_in: bfloat16 [3072, 4096], P('seq', 'chan'), may hold values from -6 to 6
- gate_in: bfloat16 [3072, 4096], P('seq', 'chan'), may hold values from -6 to 6
- gate_out: bfloat16 [3072, 4096], P('seq', 'chan'), may hold values from -6 to 6
- spectral_filter: bfloat16 [3072, 4096], P('seq', 'chan'), may hold values from -6 to 6
- analysis_blocks: bfloat16 [3, 128, 128], replicated, may hold values from -0.5 to 0.5
- analysis_mix: bfloat16 [128, 3, 3], replicated, may hold values from -3.5 to 3.5
- synthesis_blocks: bfloat16 [3, 128, 128], replicated, may hold values from -0.5 to 0.5
- synthesis_mix: bfloat16 [128, 3, 3], replicated, may hold values from -3.5 to 3.5
- angles: float32 [3, 384], replicated, may hold values from -3.140625 to 3.140625
- out_weight: bfloat16 [4096, 4096], P('chan'), may hold values from -0.09375 to 0.09375
Outputs:
- projected: bfloat16 [3072, 4096], P(('seq', 'chan'))
All inputs are finite; a program needn't handle non-finite values.
Results may differ from a plain program's by a relative error of at most 0.02.
Values may be sent and summed in bfloat16 or wider, within the bound.
A program may use at most 64 MiB of HBM per device.

v0:
```python
import jax
import jax.numpy as jnp
from jax import lax
from jax.sharding import PartitionSpec as P


def from_partner(value, axis, distance):
    mask = 2**distance
    pairs = [(source, source ^ mask) for source in range(lax.axis_size(axis))]
    return lax.ppermute(value, axis, pairs)


def rotate_pair(values, partner, theta, sign):
    cosine = jnp.cos(theta)[:, None]
    sine = sign * jnp.sin(theta)[:, None]
    return (cosine * values.astype(jnp.float32) + sine * partner.astype(jnp.float32)).astype(
        jnp.bfloat16
    )


def per_device(
    value_in,
    gate_in,
    gate_out,
    spectral_filter,
    analysis_blocks,
    analysis_mix,
    synthesis_blocks,
    synthesis_mix,
    angles,
    out_weight,
):
    tokens, chans = value_in.shape
    nblocks = analysis_blocks.shape[0]
    blk = analysis_blocks.shape[1]
    mixed = (
        (gate_in.astype(jnp.float32) * value_in.astype(jnp.float32))
        .astype(jnp.bfloat16)
        .reshape(nblocks, blk, chans)
    )
    inner = jnp.einsum(
        "kij,kjc->kic", analysis_blocks, mixed, preferred_element_type=jnp.float32
    ).astype(jnp.bfloat16)
    spec = jnp.einsum(
        "ikl,lic->kic", analysis_mix, inner, preferred_element_type=jnp.float32
    ).astype(jnp.bfloat16)
    spec = spec.reshape(tokens, chans)
    count = lax.axis_size("seq")
    sections = count.bit_length() - 1
    rank = lax.axis_index("seq")
    for section in range(sections):
        sign = 1.0 - 2.0 * (rank >> section & 1).astype(jnp.float32)
        partner = from_partner(spec, "seq", section)
        spec = rotate_pair(spec, partner, angles[section], sign)
    spec = (spec.astype(jnp.float32) * spectral_filter.astype(jnp.float32)).astype(jnp.bfloat16)
    for section in reversed(range(sections)):
        sign = 2.0 * (rank >> section & 1).astype(jnp.float32) - 1.0
        partner = from_partner(spec, "seq", section)
        spec = rotate_pair(spec, partner, angles[section], sign)
    grid = spec.reshape(nblocks, blk, chans)
    spread = jnp.einsum(
        "ikl,lic->kic", synthesis_mix, grid, preferred_element_type=jnp.float32
    ).astype(jnp.bfloat16)
    conv = jnp.einsum("kij,kjc->kic", synthesis_blocks, spread, preferred_element_type=jnp.float32)
    gated = (gate_out.astype(jnp.float32) * conv.reshape(tokens, chans)).astype(jnp.bfloat16)
    return lax.psum_scatter(
        jnp.dot(gated, out_weight, preferred_element_type=jnp.float32).astype(jnp.bfloat16),
        "chan",
        scatter_dimension=0,
        tiled=True,
    )


def solution(mesh):
    placed = (
        P("seq", "chan"),
        P("seq", "chan"),
        P("seq", "chan"),
        P("seq", "chan"),
        P(),
        P(),
        P(),
        P(),
        P(),
        P("chan", None),
    )
    return jax.shard_map(
        per_device, mesh=mesh, in_specs=placed, out_specs=P(("seq", "chan"), None), check_vma=False
    )
```

profile of v0, /device:TPU:0, one launch (start us, length us, event | category | flops | bytes accessed | tf_op | source)
XLA Modules:
  0.0 217.1 jit_solution(575705384420754201)
XLA Ops:
  6.5 0.0 copy-start
  6.5 0.0 reduce-scatter.2.cloned.1.call-start
  6.5 0.9 copy.12
  7.4 1.7 multiply_convert_fusion.1
  9.1 0.0 copy-done
  9.1 0.4 convolution_convert_fusion.2
  9.6 0.9 copy.18
  10.5 0.7 fusion.1
  11.2 0.0 copy-start.4
  11.2 0.3 copy.13
  11.5 3.0 %collective-permute-start = (bf16[384,1024]{1,0:T(8,128)(2,1)S(1)}, bf16[384,1024]{1,0:T(8,128)(2,1)S(1)}, u32[]{:S(2)}, u32[]{:S(2)}) collective-permute-start(bf16[384,1024]{1,0:T(8,128)(2,1)S(1)} %bitcast.25), channel_id=1, source_target_pairs={{0,4},{4,0},{8,12},{12,8},{16,20},{20,16},{24,28},{28,24},{1,5},{5... | collective-permute-start | bytes 2359304 | tf_op jit(solution)/shard_map/ppermute | solution.py:10
  14.5 0.0 copy-done.4
  14.5 0.2 multiply_reduce_fusion
  14.7 17.4 %collective-permute-done = bf16[384,1024]{1,0:T(8,128)(2,1)S(1)} collective-permute-done((bf16[384,1024]{1,0:T(8,128)(2,1)S(1)}, bf16[384,1024]{1,0:T(8,128)(2,1)S(1)}, u32[]{:S(2)}, u32[]{:S(2)}) %collective-permute-start) | collective-permute-done | bytes 786464 | tf_op jit(solution)/shard_map/ppermute | solution.py:10
  32.0 0.3 add_convert_fusion.5
  32.4 0.0 copy-start.1
  32.4 1.9 collective-permute-start.1
  34.3 16.9 %collective-permute-done.1 = bf16[384,1024]{1,0:T(8,128)(2,1)S(1)} collective-permute-done((bf16[384,1024]{1,0:T(8,128)(2,1)S(1)}, bf16[384,1024]{1,0:T(8,128)(2,1)S(1)}, u32[]{:S(2)}, u32[]{:S(2)}) %collective-permute-start.1) | collective-permute-done | bytes 786464 | tf_op jit(solution)/shard_map/ppermute | solution.py:10
  51.2 0.3 add_convert_fusion.4
  51.5 2.6 %collective-permute-start.2 = (bf16[384,1024]{1,0:T(8,128)(2,1)S(1)}, bf16[384,1024]{1,0:T(8,128)(2,1)S(1)}, u32[]{:S(2)}, u32[]{:S(2)}) collective-permute-start(bf16[384,1024]{1,0:T(8,128)(2,1)S(1)} %add_convert_fusion.4), channel_id=1, source_target_pairs={{0,16},{4,20},{8,24},{12,28},{16,0},{20,4},{24,8},{28,12},{1,17},{... | collective-permute-start | bytes 2359304 | tf_op jit(solution)/shard_map/ppermute | solution.py:10
  54.1 33.0 %collective-permute-done.2 = bf16[384,1024]{1,0:T(8,128)(2,1)S(1)} collective-permute-done((bf16[384,1024]{1,0:T(8,128)(2,1)S(1)}, bf16[384,1024]{1,0:T(8,128)(2,1)S(1)}, u32[]{:S(2)}, u32[]{:S(2)}) %collective-permute-start.2) | collective-permute-done | bytes 786464 | tf_op jit(solution)/shard_map/ppermute | solution.py:10
  87.2 0.0 copy-done.1
  87.2 0.4 multiply_convert_fusion
  87.6 0.1 collective-permute-start.3
  87.7 36.5 %collective-permute-done.3 = bf16[384,1024]{1,0:T(8,128)(2,1)S(1)} collective-permute-done((bf16[384,1024]{1,0:T(8,128)(2,1)S(1)}, bf16[384,1024]{1,0:T(8,128)(2,1)S(1)}, u32[]{:S(2)}, u32[]{:S(2)}) %collective-permute-start.3) | collective-permute-done | bytes 786464 | tf_op jit(solution)/shard_map/ppermute | solution.py:10
  124.2 0.3 add_convert_fusion.2
  124.6 0.0 copy-start.5
  124.6 0.1 collective-permute-start.4
  124.7 18.2 %collective-permute-done.4 = bf16[384,1024]{1,0:T(8,128)(2,1)S(1)} collective-permute-done((bf16[384,1024]{1,0:T(8,128)(2,1)S(1)}, bf16[384,1024]{1,0:T(8,128)(2,1)S(1)}, u32[]{:S(2)}, u32[]{:S(2)}) %collective-permute-start.4) | collective-permute-done | bytes 786464 | tf_op jit(solution)/shard_map/ppermute | solution.py:10
  142.9 0.3 add_convert_fusion.1
  143.3 0.1 collective-permute-start.5
  143.3 0.0 copy-done.5
  143.3 0.2 copy.16
  143.5 17.1 %collective-permute-done.5 = bf16[384,1024]{1,0:T(8,128)(2,1)S(1)} collective-permute-done((bf16[384,1024]{1,0:T(8,128)(2,1)S(1)}, bf16[384,1024]{1,0:T(8,128)(2,1)S(1)}, u32[]{:S(2)}, u32[]{:S(2)}) %collective-permute-start.5) | collective-permute-done | bytes 786464 | tf_op jit(solution)/shard_map/ppermute | solution.py:10
  160.6 0.3 add_convert_fusion
  161.0 0.0 copy-start.3
  161.0 0.9 fusion.3
  161.9 0.0 copy-done.3
  161.9 0.0 copy-start.2
  161.9 0.7 fusion.6
  162.6 0.5 copy-done.2
  163.0 0.3 fusion
  163.3 8.2 %convolution_convert_fusion = bf16[384,4096]{1,0:T(8,128)(2,1)} fusion(bf16[384,1024]{1,0:T(8,128)(2,1)S(1)} %fusion, bf16[1024,4096]{1,0:T(8,128)(2,1)} %param.19), kind=kOutput, calls=%fused_computation | convolution fusion | flops 3222798336 | bytes 12320768 | tf_op jit(solution)/shard_map/dot_general | solution.py:67
  171.5 0.0 reduce-scatter.2.cloned.1.call-update
  171.5 38.7 %reduce-scatter.2.cloned.1.call-done = bf16[96,4096]{1,0:T(8,128)(2,1)} async-done(((bf16[384,4096]{1,0:T(8,128)(2,1)}), bf16[96,4096]{1,0:T(8,128)(2,1)}) %reduce-scatter.2.cloned.1.call-update) | async-done | bytes 786448 | tf_op jit(solution)/shard_map/reduce_scatter | solution.py:66
Async XLA Ops:
  6.5 2.6 %copy-start = (bf16[3,128,128]{2,1,0:T(8,128)(2,1)S(1)}, bf16[3,128,128]{2,1,0:T(8,128)(2,1)}, u32[]{:S(2)}) copy-start(bf16[3,128,128]{2,1,0:T(8,128)(2,1)} %param.14) | copy-start | bytes 294916
  6.5 203.7 %reduce-scatter.2.cloned.1.call-start = ((), (), s32[]{:S(2)}) async-start(), calls=%async_computation.1 | async-start | bytes 3932160 | tf_op jit(solution)/shard_map/reduce_scatter | solution.py:66
  11.2 3.3 %copy-start.4 = (f32[3,384]{1,0:T(4,128)S(1)}, f32[3,384]{1,0:T(4,128)}, u32[]{:S(2)}) copy-start(f32[3,384]{1,0:T(4,128)} %param.18) | copy-start | bytes 13828
  11.5 20.5 %collective-permute-start = (bf16[384,1024]{1,0:T(8,128)(2,1)S(1)}, bf16[384,1024]{1,0:T(8,128)(2,1)S(1)}, u32[]{:S(2)}, u32[]{:S(2)}) collective-permute-start(bf16[384,1024]{1,0:T(8,128)(2,1)S(1)} %bitcast.25), channel_id=1, source_target_pairs={{0,4},{4,0},{8,12},{12,8},{16,20},{20,16},{24,28},{28,24},{1,5},{5... | collective-permute-start | bytes 2359304 | tf_op jit(solution)/shard_map/ppermute | solution.py:10
  32.4 54.8 %copy-start.1 = (bf16[384,1024]{1,0:T(8,128)(2,1)S(1)}, bf16[384,1024]{1,0:T(8,128)(2,1)}, u32[]{:S(2)}) copy-start(bf16[384,1024]{1,0:T(8,128)(2,1)} %param.13) | copy-start | bytes 2359300
  32.4 18.8 %collective-permute-start.1 = (bf16[384,1024]{1,0:T(8,128)(2,1)S(1)}, bf16[384,1024]{1,0:T(8,128)(2,1)S(1)}, u32[]{:S(2)}, u32[]{:S(2)}) collective-permute-start(bf16[384,1024]{1,0:T(8,128)(2,1)S(1)} %add_convert_fusion.5), channel_id=1, source_target_pairs={{0,8},{4,12},{8,0},{12,4},{16,24},{20,28},{24,16},{28,20},{1,9},{5... | collective-permute-start | bytes 2359304 | tf_op jit(solution)/shard_map/ppermute | solution.py:10
  51.5 35.6 %collective-permute-start.2 = (bf16[384,1024]{1,0:T(8,128)(2,1)S(1)}, bf16[384,1024]{1,0:T(8,128)(2,1)S(1)}, u32[]{:S(2)}, u32[]{:S(2)}) collective-permute-start(bf16[384,1024]{1,0:T(8,128)(2,1)S(1)} %add_convert_fusion.4), channel_id=1, source_target_pairs={{0,16},{4,20},{8,24},{12,28},{16,0},{20,4},{24,8},{28,12},{1,17},{... | collective-permute-start | bytes 2359304 | tf_op jit(solution)/shard_map/ppermute | solution.py:10
  87.6 36.6 %collective-permute-start.3 = (bf16[384,1024]{1,0:T(8,128)(2,1)S(1)}, bf16[384,1024]{1,0:T(8,128)(2,1)S(1)}, u32[]{:S(2)}, u32[]{:S(2)}) collective-permute-start(bf16[384,1024]{1,0:T(8,128)(2,1)S(1)} %multiply_convert_fusion), channel_id=1, source_target_pairs={{0,16},{4,20},{8,24},{12,28},{16,0},{20,4},{24,8},{28,12},{1,17},{... | collective-permute-start | bytes 2359304 | tf_op jit(solution)/shard_map/ppermute | solution.py:10
  124.6 18.8 %copy-start.5 = (bf16[128,3,3]{0,2,1:T(4,128)(2,1)S(1)}, bf16[128,3,3]{0,2,1:T(4,128)(2,1)}, u32[]{:S(2)}) copy-start(bf16[128,3,3]{0,2,1:T(4,128)(2,1)} %param.17) | copy-start | bytes 6916
  124.6 18.3 %collective-permute-start.4 = (bf16[384,1024]{1,0:T(8,128)(2,1)S(1)}, bf16[384,1024]{1,0:T(8,128)(2,1)S(1)}, u32[]{:S(2)}, u32[]{:S(2)}) collective-permute-start(bf16[384,1024]{1,0:T(8,128)(2,1)S(1)} %add_convert_fusion.2), channel_id=1, source_target_pairs={{0,8},{4,12},{8,0},{12,4},{16,24},{20,28},{24,16},{28,20},{1,9},{5... | collective-permute-start | bytes 2359304 | tf_op jit(solution)/shard_map/ppermute | solution.py:10
  143.3 17.4 %collective-permute-start.5 = (bf16[384,1024]{1,0:T(8,128)(2,1)S(1)}, bf16[384,1024]{1,0:T(8,128)(2,1)S(1)}, u32[]{:S(2)}, u32[]{:S(2)}) collective-permute-start(bf16[384,1024]{1,0:T(8,128)(2,1)S(1)} %add_convert_fusion.1), channel_id=1, source_target_pairs={{0,4},{4,0},{8,12},{12,8},{16,20},{20,16},{24,28},{28,24},{1,5},{5... | collective-permute-start | bytes 2359304 | tf_op jit(solution)/shard_map/ppermute | solution.py:10
  161.0 0.9 copy-start.3
  161.9 1.1 copy-start.2
Sparse Core Ops, SparseCore 0:
  171.7 38.5 reduce-scatter.1
where the time goes:
time: 217 us
  waiting for transfers between devices  178 us (82%)
  between operations  13.6 us (6%)
  matrix products  10.9 us (5%)
  starting transfers between devices  7.69 us (4%)
  other arithmetic  4.27 us (2%)
  local copies, waits for them, and re-layouts  2.77 us (1%)
    ppermute x6, waiting for transfers between devices, from_partner(): return lax.ppermute(value, axis, pairs)  139 us
    reduce_scatter x1, waiting for transfers between devices, per_device(): lax.psum_scatter(jnp.dot(gated, out_weight, preferred_element_type=jnp.fl...  38.7 us
    dot_general x1, matrix products, per_device(): jnp.dot(gated, out_weight, preferred_element_type=jnp.float32)  8.21 us
    ppermute x6, starting transfers between devices, from_partner(): return lax.ppermute(value, axis, pairs)  7.69 us
  transfers between devices with their start and end apart: 7, of which 7 were waited for; matrix products, arithmetic and copies ran while one was open for 0% of the time, Pallas kernels for 0%

commit v1 on v0

v1 whole, which is shorter than its diff:
```python
import functools

import jax
import jax.numpy as jnp
from jax import lax
from jax.experimental import pallas as pl
from jax.experimental.pallas import tpu as pltpu
from jax.sharding import PartitionSpec as P

MESH = pl.DeviceIdType.MESH
LANES = 128
PIECES = 3
STEP = 16
COLS = 512
F32 = jnp.float32
BF16 = jnp.bfloat16


def kernel(
    n,
    lane_groups,
    value_ref,
    gate_ref,
    filter_ref,
    gate_out_ref,
    analysis_ref,
    synthesis_ref,
    mix_ref,
    table_ref,
    weight_ref,
    out_ref,
    xsend,
    xs,
    fs,
    ysend,
    yr,
    gate_out,
    weight,
    gated,
    part,
    first,
    second_send,
    second,
    f_send,
    f_recv,
    x_send,
    x_recv,
    y_send,
    y_recv,
    local_sem,
    first_send_sem,
    first_recv_sem,
    second_send_sem,
    second_recv_sem,
):
    me = lax.axis_index("seq")
    chan = lax.axis_index("chan")
    core = lax.rem(chan, 2)
    side = chan // 2
    core_peer = chan + 1 - 2 * core
    side_peer = (1 - side) * 2 + core
    tokens = value_ref.shape[0]
    nb, blk, _ = analysis_ref.shape
    row_groups = n // lane_groups
    rows = tokens // row_groups
    piece = rows // PIECES
    sections = n.bit_length() - 1

    barrier = pltpu.get_barrier_semaphore()
    for s in range(1, n):
        pl.semaphore_signal(barrier, inc=1, device_id={"seq": me ^ s}, device_id_type=MESH)
    pl.semaphore_signal(barrier, inc=1, device_id={"chan": core_peer}, device_id_type=MESH)
    pl.semaphore_signal(barrier, inc=1, device_id={"chan": side_peer}, device_id_type=MESH)
    pl.semaphore_wait(barrier, n + 1)

    def chunk_lanes(index):
        return pl.ds(pl.multiple_of(lax.rem(index, lane_groups) * LANES, LANES), LANES)

    def chunk_row(index):
        return pl.multiple_of((index // lane_groups) * rows, STEP)

    my_row = chunk_row(me)

    for s in range(n - 1, 0, -1):
        there = me ^ s
        pltpu.make_async_remote_copy(
            src_ref=filter_ref.at[pl.ds(chunk_row(there), rows), chunk_lanes(there)],
            dst_ref=fs.at[s],
            send_sem=f_send,
            recv_sem=f_recv,
            device_id={"seq": there},
            device_id_type=MESH,
        ).start()
    own_filter = pltpu.make_async_copy(
        filter_ref.at[pl.ds(my_row, rows), chunk_lanes(me)], fs.at[0], local_sem.at[0]
    )
    own_filter.start()
    weight_copy = pltpu.make_async_copy(weight_ref, weight, local_sem.at[1])
    weight_copy.start()
    gate_copy = pltpu.make_async_copy(gate_out_ref, gate_out, local_sem.at[2])
    gate_copy.start()

    def analyse(step, carry):
        t = lane_groups - 1 - step
        lanes = pl.ds(
            pl.multiple_of((lax.rem(me, lane_groups) ^ t) * LANES, LANES), LANES
        )
        mixed = (gate_ref[:, lanes].astype(F32) * value_ref[:, lanes].astype(F32)).astype(BF16)
        inner = [
            jnp.dot(
                analysis_ref[k], mixed[k * blk : (k + 1) * blk], preferred_element_type=F32
            )
            .astype(BF16)
            .astype(F32)
            for k in range(nb)
        ]
        for k in range(nb):
            total = mix_ref[:, k * nb : k * nb + 1] * inner[0]
            for other in range(1, nb):
                at = k * nb + other
                total += mix_ref[:, at : at + 1] * inner[other]
            xsend[t, pl.ds(k * blk, blk), :] = total.astype(BF16)
        return carry

    lax.fori_loop(0, lane_groups, analyse, 0)
    xs[0] = xsend[0, pl.ds(my_row, rows), :]
    for p in range(PIECES):
        for s in range(n - 1, 0, -1):
            there = me ^ s
            pltpu.make_async_remote_copy(
                src_ref=xsend.at[
                    s % lane_groups,
                    pl.ds(pl.multiple_of(chunk_row(there) + p * piece, STEP), piece),
                ],
                dst_ref=xs.at[s, pl.ds(p * piece, piece)],
                send_sem=x_send.at[p],
                recv_sem=x_recv.at[p],
                device_id={"seq": there},
                device_id_type=MESH,
            ).start()

    def others(ref, p):
        return ref.at[pl.ds(1, n - 1), pl.ds(p * piece, piece)]

    def wait_bytes(ref, sem):
        pltpu.make_async_copy(ref, ref, sem).wait()

    own_filter.wait()
    wait_bytes(fs.at[pl.ds(1, n - 1)], f_recv)
    for p in range(PIECES):
        wait_bytes(others(xs, p), x_recv.at[p])

        def rotate(step, carry):
            at = pl.multiple_of(p * piece + step * STEP, STEP)
            here = pl.multiple_of(my_row + at, STEP)
            spec = [xs[s, pl.ds(at, STEP), :].astype(F32) for s in range(n)]
            cosine = [table_ref[pl.ds(here, STEP), b : b + 1] for b in range(sections)]
            sine = [
                table_ref[pl.ds(here, STEP), sections + b : sections + b + 1]
                for b in range(sections)
            ]

            def section(spec, b, flip):
                plus, minus = (sine[b], -sine[b]) if flip > 0 else (-sine[b], sine[b])
                return [
                    cosine[b] * spec[s] + (minus if s >> b & 1 else plus) * spec[s ^ (1 << b)]
                    for s in range(n)
                ]

            for b in range(sections):
                spec = section(spec, b, 1)
            spec = [spec[s] * fs[s, pl.ds(at, STEP), :].astype(F32) for s in range(n)]
            for b in reversed(range(sections)):
                spec = section(spec, b, -1)
            yr[0, pl.ds(here, STEP), :] = spec[0].astype(BF16)
            for s in range(1, n):
                ysend[s, pl.ds(at, STEP), :] = spec[s].astype(BF16)
            return carry

        lax.fori_loop(0, piece // STEP, rotate, 0)
        for s in range(n - 1, 0, -1):
            pltpu.make_async_remote_copy(
                src_ref=ysend.at[s, pl.ds(p * piece, piece)],
                dst_ref=yr.at[
                    s % lane_groups, pl.ds(pl.multiple_of(my_row + p * piece, STEP), piece)
                ],
                send_sem=y_send.at[p],
                recv_sem=y_recv.at[p],
                device_id={"seq": me ^ s},
                device_id_type=MESH,
            ).start()

    gate_copy.wait()
    for p in range(PIECES):
        wait_bytes(others(ysend, p), y_recv.at[p])

    def synthesise(t, carry):
        lanes = pl.ds(
            pl.multiple_of((lax.rem(me, lane_groups) ^ t) * LANES, LANES), LANES
        )
        back = [yr[t, pl.ds(k * blk, blk), :].astype(F32) for k in range(nb)]
        for k in range(nb):
            at = nb * nb + k * nb
            total = mix_ref[:, at : at + 1] * back[0]
            for other in range(1, nb):
                total += mix_ref[:, at + other : at + other + 1] * back[other]
            conv = jnp.dot(synthesis_ref[k], total.astype(BF16), preferred_element_type=F32)
            gated[pl.ds(k * blk, blk), lanes] = (
                gate_out[pl.ds(k * blk, blk), lanes].astype(F32) * conv
            ).astype(BF16)
        return carry

    lax.fori_loop(0, lane_groups, synthesise, 0)
    weight_copy.wait()

    share = tokens // 4
    blocks = weight.shape[1] // COLS

    def columns(q):
        return pl.ds(pl.multiple_of(q * COLS, COLS), COLS)

    def to_core(q):
        return pltpu.make_async_remote_copy(
            src_ref=part.at[q, 1 - core],
            dst_ref=first.at[q],
            send_sem=first_send_sem.at[q],
            recv_sem=first_recv_sem.at[q],
            device_id={"chan": core_peer},
            device_id_type=MESH,
        )

    def to_side(q):
        return pltpu.make_async_remote_copy(
            src_ref=second_send.at[q],
            dst_ref=second.at[q],
            send_sem=second_send_sem.at[q],
            recv_sem=second_recv_sem.at[q],
            device_id={"chan": side_peer},
            device_id_type=MESH,
        )

    def forward(q):
        to_core(q).wait_recv()
        second_send[q] = (
            part[q, core, 1 - side].astype(F32) + first[q, 1 - side].astype(F32)
        ).astype(BF16)
        to_side(q).start()

    def project(q, carry):
        product = jnp.dot(gated[...], weight[:, columns(q)], preferred_element_type=F32)
        for g in range(4):
            part[q, g % 2, g // 2] = product[g * share : (g + 1) * share].astype(BF16)
        to_core(q).start()

        @pl.when(q > 0)
        def _():
            forward(q - 1)

        return carry

    lax.fori_loop(0, blocks, project, 0)
    forward(blocks - 1)

    def finish(q, carry):
        to_side(q).wait_recv()
        out_ref[:, columns(q)] = (
            part[q, core, side].astype(F32)
            + first[q, side].astype(F32)
            + second[q].astype(F32)
        ).astype(BF16)
        to_core(q).wait_send()
        to_side(q).wait_send()
        return carry

    lax.fori_loop(0, blocks, finish, 0)
    wait_bytes(fs.at[pl.ds(1, n - 1)], f_send)
    for p in range(PIECES):
        wait_bytes(others(xs, p), x_send.at[p])
        wait_bytes(others(ysend, p), y_send.at[p])


def per_device(
    value_in,
    gate_in,
    gate_out,
    spectral_filter,
    analysis_blocks,
    analysis_mix,
    synthesis_blocks,
    synthesis_mix,
    angles,
    out_weight,
):
    tokens, chans = value_in.shape
    blk = analysis_blocks.shape[1]
    width = out_weight.shape[1]
    n = lax.axis_size("seq")
    sections = n.bit_length() - 1
    lane_groups = min(n, chans // LANES)
    rows = tokens // (n // lane_groups)
    blocks = width // COLS
    share = tokens // 4
    bit = lax.axis_index("seq") >> jnp.arange(sections) & 1
    sign = (1 - 2 * bit).astype(F32)[:, None]
    table = jnp.concatenate([jnp.cos(angles), sign * jnp.sin(angles)], axis=0).T
    mix = jnp.concatenate(
        [analysis_mix.reshape(blk, -1), synthesis_mix.reshape(blk, -1)], axis=1
    ).astype(F32)
    vmem = pl.BlockSpec(memory_space=pltpu.VMEM)
    anywhere = pl.BlockSpec(memory_space=pl.ANY)
    chunk = pltpu.VMEM((n, rows, LANES), BF16)
    whole = pltpu.VMEM((lane_groups, tokens, LANES), BF16)
    return pl.pallas_call(
        functools.partial(kernel, n, lane_groups),
        out_shape=jax.ShapeDtypeStruct((share, width), BF16),
        in_specs=[vmem, vmem, anywhere, anywhere, vmem, vmem, vmem, vmem, anywhere],
        out_specs=vmem,
        scratch_shapes=[
            whole,
            chunk,
            chunk,
            chunk,
            whole,
            pltpu.VMEM((tokens, chans), BF16),
            pltpu.VMEM(out_weight.shape, BF16),
            pltpu.VMEM((tokens, chans), BF16),
            pltpu.VMEM((blocks, 2, 2, share, COLS), BF16),
            pltpu.VMEM((blocks, 2, share, COLS), BF16),
            pltpu.VMEM((blocks, share, COLS), BF16),
            pltpu.VMEM((blocks, share, COLS), BF16),
            pltpu.SemaphoreType.DMA,
            pltpu.SemaphoreType.DMA,
            pltpu.SemaphoreType.DMA((PIECES,)),
            pltpu.SemaphoreType.DMA((PIECES,)),
            pltpu.SemaphoreType.DMA((PIECES,)),
            pltpu.SemaphoreType.DMA((PIECES,)),
            pltpu.SemaphoreType.DMA((3,)),
            pltpu.SemaphoreType.DMA((blocks,)),
            pltpu.SemaphoreType.DMA((blocks,)),
            pltpu.SemaphoreType.DMA((blocks,)),
            pltpu.SemaphoreType.DMA((blocks,)),
        ],
        compiler_params=pltpu.CompilerParams(
            collective_id=0, has_side_effects=True, vmem_limit_bytes=48 * 2**20
        ),
    )(
        value_in,
        gate_in,
        spectral_filter,
        gate_out,
        analysis_blocks,
        synthesis_blocks,
        mix,
        table,
        out_weight,
    )


def solution(mesh):
    placed = (
        P("seq", "chan"),
        P("seq", "chan"),
        P("seq", "chan"),
        P("seq", "chan"),
        P(),
        P(),
        P(),
        P(),
        P(),
        P("chan", None),
    )
    return jax.shard_map(
        per_device, mesh=mesh, in_specs=placed, out_specs=P(("seq", "chan"), None), check_vma=False
    )
```

time: 217 us -> 92.8 us (0.43)
  waiting for transfers between devices: 178 us -> 0 us
  Pallas kernels: 0 us -> 82.7 us
  between operations: 13.6 us -> 0.04 us
  matrix products: 10.9 us -> 0 us
  starting transfers between devices: 7.69 us -> 0 us
  local copies, waits for them, and re-layouts: 2.77 us -> 8.84 us
  other arithmetic: 4.27 us -> 0.78 us
    ppermute x6 -> x0, waiting for transfers between devices: 139 us -> none  [from_partner(): return lax.ppermute(value, axis, pairs)]
    pallas_call x0 -> x1, Pallas kernels: none -> 82.7 us  [per_device(): pl.pallas_call(functools.partial(kernel, n, lane_groups), out_shape=jax.S...]
    reduce_scatter x1 -> x0, waiting for transfers between devices: 38.7 us -> none  [per_device(): lax.psum_scatter(jnp.dot(gated, out_weight, preferred_element_type=jnp.fl...]
    dot_general x5 -> x0, matrix products: 10.9 us -> none  [the longest x1 8.21 us: per_device(): jnp.dot(gated, out_weight, preferred_element_type=jnp.float32)]
    ppermute x6 -> x0, starting transfers between devices: 7.69 us -> none  [from_partner(): return lax.ppermute(value, axis, pairs)]
    unnamed x15 -> x13, local copies, waits for them, and re-layouts: 2.46 us -> 7.2 us
    convert_element_type x8 -> x2, other arithmetic: 4.09 us -> 0.02 us  [the longest x1 0.01 us: per_device(): mix = jnp.concatenate([analysis_mix.reshape(blk, -1), synthesis_mix.resha...]
  transfers between devices with their start and end apart: 7 -> 0, of which waited for: 7 -> 0; matrix products, arithmetic and copies ran while one was open for 0% -> 0% of each run, Pallas kernels for 0% -> 0%
where the time goes in v1:
time: 92.8 us; the launch traced here: 92.4 us
  Pallas kernels  82.7 us (89%)
  local copies, waits for them, and re-layouts  8.84 us (10%)
    pallas_call x1, Pallas kernels, per_device(): pl.pallas_call(functools.partial(kernel, n, lane_groups), out_shape=jax.S...  82.7 us
    unnamed x13, local copies, waits for them, and re-layouts  7.2 us

profile of v1, /device:TPU:0, one launch (start us, length us, event | category | flops | bytes accessed | tf_op | source)
XLA Modules:
  0.0 92.4 jit_solution(16865145058855228201)
XLA Ops:
  0.0 0.7 reshape.14
  0.7 0.7 reshape.15
  1.4 0.8 fusion
  2.2 0.1 copy.22.mix_ref
  2.3 0.1 copy.21
  2.4 0.0 copy-start
  2.5 1.1 %copy-done = bf16[384,1024]{1,0:T(8,128)(2,1)S(1)} copy-done((bf16[384,1024]{1,0:T(8,128)(2,1)S(1)}, bf16[384,1024]{1,0:T(8,128)(2,1)}, u32[]{:S(2)}) %copy-start) | copy-done | bytes 786456
  3.6 0.0 copy-start.1
  3.6 1.1 %copy-done.1 = bf16[384,1024]{1,0:T(8,128)(2,1)S(1)} copy-done((bf16[384,1024]{1,0:T(8,128)(2,1)S(1)}, bf16[384,1024]{1,0:T(8,128)(2,1)}, u32[]{:S(2)}) %copy-start.1) | copy-done | bytes 786456
  4.7 0.0 copy-start.2
  4.7 1.1 %copy-done.2 = bf16[384,1024]{1,0:T(8,128)(2,1)S(1)} copy-done((bf16[384,1024]{1,0:T(8,128)(2,1)S(1)}, bf16[384,1024]{1,0:T(8,128)(2,1)}, u32[]{:S(2)}) %copy-start.2) | copy-done | bytes 786456
  5.8 0.0 copy-start.3
  5.9 1.1 %copy-done.3 = bf16[384,1024]{1,0:T(8,128)(2,1)S(1)} copy-done((bf16[384,1024]{1,0:T(8,128)(2,1)S(1)}, bf16[384,1024]{1,0:T(8,128)(2,1)}, u32[]{:S(2)}) %copy-start.3) | copy-done | bytes 786456
  7.0 0.0 copy-start.4
  7.0 0.9 copy-done.4
  7.9 0.0 copy-start.5
  7.9 0.9 copy-done.5
  8.8 82.7 %shard_map.100 = bf16[96,4096]{1,0:T(8,128)(2,1)S(1)} custom-call(bf16[384,1024]{1,0:T(8,128)(2,1)S(1)} %copy-done, bf16[384,1024]{1,0:T(8,128)(2,1)S(1)} %copy-done.1, bf16[384,1024]{1,0:T(8,128)(2,1)S(1)} %copy-done.2, bf16[384,1024]{1,0:T(8,128)(2,1)S(1)} %copy-done.3, bf16[3,128,128]{2,1,0:T(8,128)(2,1)S(1)} %copy-done.4, ...), custom_call_target="tpu_custom_call" | custom-call | tf_op jit(solution)/shard_map/pallas_call | solution.py:313
  91.5 0.9 copy.24
  (3 shorter events, 0.0 us)
Async XLA Ops:
  2.4 1.1 %copy-start = (bf16[384,1024]{1,0:T(8,128)(2,1)S(1)}, bf16[384,1024]{1,0:T(8,128)(2,1)}, u32[]{:S(2)}) copy-start(bf16[384,1024]{1,0:T(8,128)(2,1)} %value_ref.1) | copy-start | bytes 2359300
  3.6 1.1 %copy-start.1 = (bf16[384,1024]{1,0:T(8,128)(2,1)S(1)}, bf16[384,1024]{1,0:T(8,128)(2,1)}, u32[]{:S(2)}) copy-start(bf16[384,1024]{1,0:T(8,128)(2,1)} %gate_ref.1) | copy-start | bytes 2359300
  4.7 1.1 %copy-start.2 = (bf16[384,1024]{1,0:T(8,128)(2,1)S(1)}, bf16[384,1024]{1,0:T(8,128)(2,1)}, u32[]{:S(2)}) copy-start(bf16[384,1024]{1,0:T(8,128)(2,1)} %filter_ref.1) | copy-start | bytes 2359300
  5.8 1.1 %copy-start.3 = (bf16[384,1024]{1,0:T(8,128)(2,1)S(1)}, bf16[384,1024]{1,0:T(8,128)(2,1)}, u32[]{:S(2)}) copy-start(bf16[384,1024]{1,0:T(8,128)(2,1)} %gate_out_ref.1) | copy-start | bytes 2359300
  7.0 0.9 copy-start.4
  7.9 0.9 copy-start.5

commit v2 on v1

--- a/solution.py
+++ b/solution.py
@@ -19,16 +19,27 @@
 def kernel(
     n,
     lane_groups,
+    value_hbm,
+    gate_hbm,
+    filter_ref,
+    gate_out_ref,
+    analysis_hbm,
+    synthesis_hbm,
+    analysis_mix_hbm,
+    synthesis_mix_hbm,
+    angles_hbm,
+    weight_ref,
+    out_ref,
     value_ref,
     gate_ref,
-    filter_ref,
-    gate_out_ref,
     analysis_ref,
     synthesis_ref,
+    analysis_mix,
+    synthesis_mix,
+    angles,
     mix_ref,
     table_ref,
-    weight_ref,
-    out_ref,
+    wide,
     xsend,
     xs,
     fs,
@@ -48,6 +59,7 @@
     y_send,
     y_recv,
     local_sem,
+    load_sem,
     first_send_sem,
     first_recv_sem,
     second_send_sem,
@@ -59,12 +71,29 @@
     side = chan // 2
     core_peer = chan + 1 - 2 * core
     side_peer = (1 - side) * 2 + core
-    tokens = value_ref.shape[0]
-    nb, blk, _ = analysis_ref.shape
+    tokens = value_hbm.shape[0]
+    nb, blk, _ = analysis_hbm.shape
     row_groups = n // lane_groups
     rows = tokens // row_groups
     piece = rows // PIECES
     sections = n.bit_length() - 1
+
+    loads = [
+        pltpu.make_async_copy(source, target, load_sem.at[at])
+        for at, (source, target) in enumerate(
+            (
+                (value_hbm, value_ref),
+                (gate_hbm, gate_ref),
+                (analysis_hbm, analysis_ref),
+                (analysis_mix_hbm, analysis_mix),
+                (synthesis_mix_hbm, synthesis_mix),
+                (angles_hbm, angles),
+                (synthesis_hbm, synthesis_ref),
+            )
+        )
+    ]
+    for load in loads:
+        load.start()
 
     barrier = pltpu.get_barrier_semaphore()
     for s in range(1, n):
@@ -99,6 +128,16 @@
     weight_copy.start()
     gate_copy = pltpu.make_async_copy(gate_out_ref, gate_out, local_sem.at[2])
     gate_copy.start()
+
+    for load in loads:
+        load.wait()
+
+    wide[...] = jnp.zeros_like(wide)
+    for which, source in enumerate((analysis_mix, synthesis_mix)):
+        for k in range(nb):
+            at = (which * nb + k) * nb
+            wide[pl.ds(at, nb), :] = source[k].astype(F32)
+    mix_ref[...] = wide[...].T
 
     def analyse(step, carry):
         t = lane_groups - 1 - step
@@ -139,6 +178,15 @@
                 device_id_type=MESH,
             ).start()
 
+    for k in range(nb):
+        theta = angles[:, pl.ds(k * blk, blk)]
+        cosine, sine = jnp.cos(theta), jnp.sin(theta)
+        for b in range(sections):
+            sign = (1 - 2 * (me >> b & 1)).astype(F32)
+            wide[pl.ds(b, 1), :] = cosine[b : b + 1]
+            wide[pl.ds(sections + b, 1), :] = sine[b : b + 1] * sign
+        table_ref[pl.ds(k * blk, blk), :] = wide[...].T
+
     def others(ref, p):
         return ref.at[pl.ds(1, n - 1), pl.ds(p * piece, piece)]
 
@@ -185,16 +233,20 @@
                     s % lane_groups, pl.ds(pl.multiple_of(my_row + p * piece, STEP), piece)
                 ],
                 send_sem=y_send.at[p],
-                recv_sem=y_recv.at[p],
+                recv_sem=y_recv.at[s],
                 device_id={"seq": me ^ s},
                 device_id_type=MESH,
             ).start()
 
     gate_copy.wait()
-    for p in range(PIECES):
-        wait_bytes(others(ysend, p), y_recv.at[p])
 
     def synthesise(t, carry):
+        @pl.when(t > 0)
+        def _():
+            wait_bytes(ysend.at[t], y_recv.at[t])
+
+        for u in range(1, row_groups):
+            wait_bytes(ysend.at[u * lane_groups + t], y_recv.at[u * lane_groups + t])
         lanes = pl.ds(
             pl.multiple_of((lax.rem(me, lane_groups) ^ t) * LANES, LANES), LANES
         )
@@ -292,30 +344,35 @@
     out_weight,
 ):
     tokens, chans = value_in.shape
+    analysis_mix = analysis_mix.transpose(1, 2, 0)
+    synthesis_mix = synthesis_mix.transpose(1, 2, 0)
     blk = analysis_blocks.shape[1]
     width = out_weight.shape[1]
     n = lax.axis_size("seq")
-    sections = n.bit_length() - 1
     lane_groups = min(n, chans // LANES)
     rows = tokens // (n // lane_groups)
     blocks = width // COLS
     share = tokens // 4
-    bit = lax.axis_index("seq") >> jnp.arange(sections) & 1
-    sign = (1 - 2 * bit).astype(F32)[:, None]
-    table = jnp.concatenate([jnp.cos(angles), sign * jnp.sin(angles)], axis=0).T
-    mix = jnp.concatenate(
-        [analysis_mix.reshape(blk, -1), synthesis_mix.reshape(blk, -1)], axis=1
-    ).astype(F32)
     vmem = pl.BlockSpec(memory_space=pltpu.VMEM)
-    anywhere = pl.BlockSpec(memory_space=pl.ANY)
+    hbm = pl.BlockSpec(memory_space=pltpu.HBM)
     chunk = pltpu.VMEM((n, rows, LANES), BF16)
     whole = pltpu.VMEM((lane_groups, tokens, LANES), BF16)
     return pl.pallas_call(
         functools.partial(kernel, n, lane_groups),
         out_shape=jax.ShapeDtypeStruct((share, width), BF16),
-        in_specs=[vmem, vmem, anywhere, anywhere, vmem, vmem, vmem, vmem, anywhere],
+        in_specs=[hbm] * 10,
         out_specs=vmem,
         scratch_shapes=[
+            pltpu.VMEM((tokens, chans), BF16),
+            pltpu.VMEM((tokens, chans), BF16),
+            pltpu.VMEM(analysis_blocks.shape, BF16),
+            pltpu.VMEM(synthesis_blocks.shape, BF16),
+            pltpu.VMEM(analysis_mix.shape, BF16),
+            pltpu.VMEM(synthesis_mix.shape, BF16),
+            pltpu.VMEM(angles.shape, F32),
+            pltpu.VMEM((blk, LANES), F32),
+            pltpu.VMEM((tokens, LANES), F32),
+            pltpu.VMEM((LANES, blk), F32),
             whole,
             chunk,
             chunk,
@@ -333,15 +390,16 @@
             pltpu.SemaphoreType.DMA((PIECES,)),
             pltpu.SemaphoreType.DMA((PIECES,)),
             pltpu.SemaphoreType.DMA((PIECES,)),
-            pltpu.SemaphoreType.DMA((PIECES,)),
+            pltpu.SemaphoreType.DMA((n,)),
             pltpu.SemaphoreType.DMA((3,)),
+            pltpu.SemaphoreType.DMA((7,)),
             pltpu.SemaphoreType.DMA((blocks,)),
             pltpu.SemaphoreType.DMA((blocks,)),
             pltpu.SemaphoreType.DMA((blocks,)),
             pltpu.SemaphoreType.DMA((blocks,)),
         ],
         compiler_params=pltpu.CompilerParams(
-            collective_id=0, has_side_effects=True, vmem_limit_bytes=48 * 2**20
+            collective_id=0, has_side_effects=True, vmem_limit_bytes=62 * 2**20
         ),
     )(
         value_in,
@@ -350,8 +408,9 @@
         gate_out,
         analysis_blocks,
         synthesis_blocks,
-        mix,
-        table,
+        analysis_mix,
+        synthesis_mix,
+        angles,
         out_weight,
     )
 

time: 92.8 us -> 84.5 us (0.911)
  local copies, waits for them, and re-layouts: 8.84 us -> 2.06 us
    unnamed x13 -> x1, local copies, waits for them, and re-layouts: 7.2 us -> 2.06 us
    reshape x2 -> x0, local copies, waits for them, and re-layouts: 1.4 us -> none  [the longest x1 0.7 us: per_device(): analysis_mix.reshape(blk, -1)]
where the time goes in v2:
time: 84.5 us; the launch traced here: 84.3 us
  Pallas kernels  82.2 us (97%)
  local copies, waits for them, and re-layouts  2.06 us (2%)
    pallas_call x1, Pallas kernels, per_device(): pl.pallas_call(functools.partial(kernel, n, lane_groups), out_shape=jax.S...  82.2 us
    unnamed x1, local copies, waits for them, and re-layouts  2.06 us

profile of v2, /device:TPU:0, one launch (start us, length us, event | category | flops | bytes accessed | tf_op | source)
XLA Modules:
  0.0 84.3 jit_solution(5096457500570303871)
XLA Ops:
  0.0 82.2 %shard_map.100 = bf16[96,4096]{1,0:T(8,128)(2,1)} custom-call(bf16[384,1024]{1,0:T(8,128)(2,1)} %value_hbm.1, bf16[384,1024]{1,0:T(8,128)(2,1)} %gate_hbm.1, bf16[384,1024]{1,0:T(8,128)(2,1)} %filter_ref.1, bf16[384,1024]{1,0:T(8,128)(2,1)} %gate_out_ref.1, bf16[3,128,128]{2,1,0:T(8,128)(2,1)} %analysis_hbm.1, bf16[3,128,128]{2,1,0:T(8,128)(2,1)} %synthesis_hbm.1, ...), custom_call_target="tpu_custom_call" | custom-call | tf_op jit(solution)/shard_map/pallas_call | solution.py:360
  82.2 2.1 %copy.12 = bf16[96,4096]{1,0:T(8,128)(2,1)} copy(bf16[96,4096]{1,0:T(8,128)(2,1)} %shard_map.100) | data formatting | bytes 1572864

commit v3 on v2

--- a/solution.py
+++ b/solution.py
@@ -11,7 +11,7 @@
 LANES = 128
 PIECES = 3
 STEP = 16
-COLS = 512
+COLS = 256
 F32 = jnp.float32
 BF16 = jnp.bfloat16
 
@@ -29,7 +29,8 @@
     synthesis_mix_hbm,
     angles_hbm,
     weight_ref,
-    out_ref,
+    own_ref,
+    second,
     value_ref,
     gate_ref,
     analysis_ref,
@@ -51,7 +52,7 @@
     part,
     first,
     second_send,
-    second,
+    own,
     f_send,
     f_recv,
     x_send,
@@ -64,6 +65,7 @@
     first_recv_sem,
     second_send_sem,
     second_recv_sem,
+    own_sem,
 ):
     me = lax.axis_index("seq")
     chan = lax.axis_index("chan")
@@ -284,12 +286,15 @@
     def to_side(q):
         return pltpu.make_async_remote_copy(
             src_ref=second_send.at[q],
-            dst_ref=second.at[q],
+            dst_ref=second.at[:, columns(q)],
             send_sem=second_send_sem.at[q],
             recv_sem=second_recv_sem.at[q],
             device_id={"chan": side_peer},
             device_id_type=MESH,
         )
+
+    def keep(q):
+        return pltpu.make_async_copy(own.at[q], own_ref.at[:, columns(q)], own_sem.at[q])
 
     def forward(q):
         to_core(q).wait_recv()
@@ -297,6 +302,8 @@
             part[q, core, 1 - side].astype(F32) + first[q, 1 - side].astype(F32)
         ).astype(BF16)
         to_side(q).start()
+        own[q] = (part[q, core, side].astype(F32) + first[q, side].astype(F32)).astype(BF16)
+        keep(q).start()
 
     def project(q, carry):
         product = jnp.dot(gated[...], weight[:, columns(q)], preferred_element_type=F32)
@@ -315,11 +322,7 @@
 
     def finish(q, carry):
         to_side(q).wait_recv()
-        out_ref[:, columns(q)] = (
-            part[q, core, side].astype(F32)
-            + first[q, side].astype(F32)
-            + second[q].astype(F32)
-        ).astype(BF16)
+        keep(q).wait()
         to_core(q).wait_send()
         to_side(q).wait_send()
         return carry
@@ -353,15 +356,14 @@
     rows = tokens // (n // lane_groups)
     blocks = width // COLS
     share = tokens // 4
-    vmem = pl.BlockSpec(memory_space=pltpu.VMEM)
     hbm = pl.BlockSpec(memory_space=pltpu.HBM)
     chunk = pltpu.VMEM((n, rows, LANES), BF16)
     whole = pltpu.VMEM((lane_groups, tokens, LANES), BF16)
-    return pl.pallas_call(
+    own, other = pl.pallas_call(
         functools.partial(kernel, n, lane_groups),
-        out_shape=jax.ShapeDtypeStruct((share, width), BF16),
+        out_shape=[jax.ShapeDtypeStruct((share, width), BF16)] * 2,
         in_specs=[hbm] * 10,
-        out_specs=vmem,
+        out_specs=[hbm] * 2,
         scratch_shapes=[
             pltpu.VMEM((tokens, chans), BF16),
             pltpu.VMEM((tokens, chans), BF16),
@@ -397,6 +399,7 @@
             pltpu.SemaphoreType.DMA((blocks,)),
             pltpu.SemaphoreType.DMA((blocks,)),
             pltpu.SemaphoreType.DMA((blocks,)),
+            pltpu.SemaphoreType.DMA((blocks,)),
         ],
         compiler_params=pltpu.CompilerParams(
             collective_id=0, has_side_effects=True, vmem_limit_bytes=62 * 2**20
@@ -413,6 +416,7 @@
         angles,
         out_weight,
     )
+    return (own.astype(F32) + other.astype(F32)).astype(BF16)
 
 
 def solution(mesh):

time: 84.5 us -> 84.1 us (level)
  other arithmetic: 0 us -> 2.45 us
  local copies, waits for them, and re-layouts: 2.06 us -> 0 us
    convert_element_type x0 -> x1, other arithmetic: none -> 2.45 us  [per_device(): return (own.astype(F32) + other.astype(F32)).astype(BF16)]
    unnamed x1 -> x0, local copies, waits for them, and re-layouts: 2.06 us -> none
where the time goes in v3:
time: 84.1 us; the launch traced here: 84 us
  Pallas kernels  81.5 us (97%)
  other arithmetic  2.45 us (3%)
    pallas_call x1, Pallas kernels, per_device(): pl.pallas_call(functools.partial(kernel, n, lane_groups), out_shape=[jax....  81.5 us
    convert_element_type x1, other arithmetic, per_device(): return (own.astype(F32) + other.astype(F32)).astype(BF16)  2.45 us

profile of v3, /device:TPU:0, one launch (start us, length us, event | category | flops | bytes accessed | tf_op | source)
XLA Modules:
  0.0 84.0 jit_solution(18236273381937726702)
XLA Ops:
  0.0 81.5 %shard_map.100 = (bf16[96,4096]{1,0:T(8,128)(2,1)}, bf16[96,4096]{1,0:T(8,128)(2,1)}) custom-call(bf16[384,1024]{1,0:T(8,128)(2,1)} %value_hbm.1, bf16[384,1024]{1,0:T(8,128)(2,1)} %gate_hbm.1, bf16[384,1024]{1,0:T(8,128)(2,1)} %filter_ref.1, bf16[384,1024]{1,0:T(8,128)(2,1)} %gate_out_ref.1, bf16[3,128,128]{2,1,0:T(8,128)(2,1)} %analysis_hbm.1, ...), custom_call_target="tpu_custom_call" | custom-call | tf_op jit(solution)/shard_map/pallas_call | solution.py:362
  81.5 2.4 %add_convert_fusion = bf16[96,4096]{1,0:T(8,128)(2,1)} fusion(bf16[96,4096]{1,0:T(8,128)(2,1)} %get-tuple-element.8, bf16[96,4096]{1,0:T(8,128)(2,1)} %get-tuple-element.7), kind=kLoop, calls=%fused_computation | loop fusion | flops 1572864 | bytes 2359296 | tf_op jit(solution)/shard_map/convert_element_type | solution.py:419

commit v4 on v2

--- a/solution.py
+++ b/solution.py
@@ -95,6 +95,13 @@
     for load in loads:
         load.start()
 
+    order = [
+        s
+        for step in range(n // 2)
+        for s in (n - 1 - step, n // 2 - 1 - step)
+        if s > 0
+    ]
+
     barrier = pltpu.get_barrier_semaphore()
     for s in range(1, n):
         pl.semaphore_signal(barrier, inc=1, device_id={"seq": me ^ s}, device_id_type=MESH)
@@ -110,7 +117,7 @@
 
     my_row = chunk_row(me)
 
-    for s in range(n - 1, 0, -1):
+    for s in order:
         there = me ^ s
         pltpu.make_async_remote_copy(
             src_ref=filter_ref.at[pl.ds(chunk_row(there), rows), chunk_lanes(there)],
@@ -164,7 +171,7 @@
     lax.fori_loop(0, lane_groups, analyse, 0)
     xs[0] = xsend[0, pl.ds(my_row, rows), :]
     for p in range(PIECES):
-        for s in range(n - 1, 0, -1):
+        for s in order:
             there = me ^ s
             pltpu.make_async_remote_copy(
                 src_ref=xsend.at[
@@ -226,7 +233,7 @@
             return carry
 
         lax.fori_loop(0, piece // STEP, rotate, 0)
-        for s in range(n - 1, 0, -1):
+        for s in order:
             pltpu.make_async_remote_copy(
                 src_ref=ysend.at[s, pl.ds(p * piece, piece)],
                 dst_ref=yr.at[

time: 84.5 us -> 84.4 us (level)
  no operation moved by 1% of the time
where the time goes in v4:
time: 84.4 us; the launch traced here: 84.3 us
  Pallas kernels  82.2 us (97%)
  local copies, waits for them, and re-layouts  2.06 us (2%)
    pallas_call x1, Pallas kernels, per_device(): pl.pallas_call(functools.partial(kernel, n, lane_groups), out_shape=jax.S...  82.2 us
    unnamed x1, local copies, waits for them, and re-layouts  2.06 us

profile of v4, /device:TPU:0, one launch (start us, length us, event | category | flops | bytes accessed | tf_op | source)
XLA Modules:
  0.0 84.3 jit_solution(15669600640281416705)
XLA Ops:
  0.0 82.2 %shard_map.100 = bf16[96,4096]{1,0:T(8,128)(2,1)} custom-call(bf16[384,1024]{1,0:T(8,128)(2,1)} %value_hbm.1, bf16[384,1024]{1,0:T(8,128)(2,1)} %gate_hbm.1, bf16[384,1024]{1,0:T(8,128)(2,1)} %filter_ref.1, bf16[384,1024]{1,0:T(8,128)(2,1)} %gate_out_ref.1, bf16[3,128,128]{2,1,0:T(8,128)(2,1)} %analysis_hbm.1, bf16[3,128,128]{2,1,0:T(8,128)(2,1)} %synthesis_hbm.1, ...), custom_call_target="tpu_custom_call" | custom-call | tf_op jit(solution)/shard_map/pallas_call | solution.py:367
  82.2 2.1 %copy.12 = bf16[96,4096]{1,0:T(8,128)(2,1)} copy(bf16[96,4096]{1,0:T(8,128)(2,1)} %shard_map.100) | data formatting | bytes 1572864

commit v5 on v2

--- a/solution.py
+++ b/solution.py
@@ -163,7 +163,8 @@
 
     lax.fori_loop(0, lane_groups, analyse, 0)
     xs[0] = xsend[0, pl.ds(my_row, rows), :]
-    for p in range(PIECES):
+
+    def send_piece(p):
         for s in range(n - 1, 0, -1):
             there = me ^ s
             pltpu.make_async_remote_copy(
@@ -178,6 +179,7 @@
                 device_id_type=MESH,
             ).start()
 
+    send_piece(0)
     for k in range(nb):
         theta = angles[:, pl.ds(k * blk, blk)]
         cosine, sine = jnp.cos(theta), jnp.sin(theta)
@@ -195,8 +197,11 @@
 
     own_filter.wait()
     wait_bytes(fs.at[pl.ds(1, n - 1)], f_recv)
+    send_piece(1)
     for p in range(PIECES):
         wait_bytes(others(xs, p), x_recv.at[p])
+        if p + 2 < PIECES:
+            send_piece(p + 2)
 
         def rotate(step, carry):
             at = pl.multiple_of(p * piece + step * STEP, STEP)

time: 84.5 us -> 84.4 us (level)
  no operation moved by 1% of the time
where the time goes in v5:
time: 84.4 us; the launch traced here: 84.2 us
  Pallas kernels  82.2 us (97%)
  local copies, waits for them, and re-layouts  2.06 us (2%)
    pallas_call x1, Pallas kernels, per_device(): pl.pallas_call(functools.partial(kernel, n, lane_groups), out_shape=jax.S...  82.2 us
    unnamed x1, local copies, waits for them, and re-layouts  2.06 us

profile of v5, /device:TPU:0, one launch (start us, length us, event | category | flops | bytes accessed | tf_op | source)
XLA Modules:
  0.0 84.2 jit_solution(7782642872163681678)
XLA Ops:
  0.0 82.2 %shard_map.100 = bf16[96,4096]{1,0:T(8,128)(2,1)} custom-call(bf16[384,1024]{1,0:T(8,128)(2,1)} %value_hbm.1, bf16[384,1024]{1,0:T(8,128)(2,1)} %gate_hbm.1, bf16[384,1024]{1,0:T(8,128)(2,1)} %filter_ref.1, bf16[384,1024]{1,0:T(8,128)(2,1)} %gate_out_ref.1, bf16[3,128,128]{2,1,0:T(8,128)(2,1)} %analysis_hbm.1, bf16[3,128,128]{2,1,0:T(8,128)(2,1)} %synthesis_hbm.1, ...), custom_call_target="tpu_custom_call" | custom-call | tf_op jit(solution)/shard_map/pallas_call | solution.py:365
  82.2 2.1 %copy.12 = bf16[96,4096]{1,0:T(8,128)(2,1)} copy(bf16[96,4096]{1,0:T(8,128)(2,1)} %shard_map.100) | data formatting | bytes 1572864

commit v6 on v2

--- a/solution.py
+++ b/solution.py
@@ -240,13 +240,15 @@
 
     gate_copy.wait()
 
-    def synthesise(t, carry):
+    def arrive(t):
         @pl.when(t > 0)
         def _():
             wait_bytes(ysend.at[t], y_recv.at[t])
 
         for u in range(1, row_groups):
             wait_bytes(ysend.at[u * lane_groups + t], y_recv.at[u * lane_groups + t])
+
+    def group(t):
         lanes = pl.ds(
             pl.multiple_of((lax.rem(me, lane_groups) ^ t) * LANES, LANES), LANES
         )
@@ -260,9 +262,15 @@
             gated[pl.ds(k * blk, blk), lanes] = (
                 gate_out[pl.ds(k * blk, blk), lanes].astype(F32) * conv
             ).astype(BF16)
+
+    def synthesise(pair, carry):
+        arrive(2 * pair)
+        arrive(2 * pair + 1)
+        group(2 * pair)
+        group(2 * pair + 1)
         return carry
 
-    lax.fori_loop(0, lane_groups, synthesise, 0)
+    lax.fori_loop(0, lane_groups // 2, synthesise, 0)
     weight_copy.wait()
 
     share = tokens // 4

time: 84.5 us -> 84 us (level)
  no operation moved by 1% of the time
where the time goes in v6:
time: 84 us; the launch traced here: 83.8 us
  Pallas kernels  81.8 us (97%)
  local copies, waits for them, and re-layouts  2.06 us (2%)
    pallas_call x1, Pallas kernels, per_device(): pl.pallas_call(functools.partial(kernel, n, lane_groups), out_shape=jax.S...  81.8 us
    unnamed x1, local copies, waits for them, and re-layouts  2.06 us

profile of v6, /device:TPU:0, one launch (start us, length us, event | category | flops | bytes accessed | tf_op | source)
XLA Modules:
  0.0 83.8 jit_solution(6083049332278410787)
XLA Ops:
  0.0 81.8 %shard_map.100 = bf16[96,4096]{1,0:T(8,128)(2,1)} custom-call(bf16[384,1024]{1,0:T(8,128)(2,1)} %value_hbm.1, bf16[384,1024]{1,0:T(8,128)(2,1)} %gate_hbm.1, bf16[384,1024]{1,0:T(8,128)(2,1)} %filter_ref.1, bf16[384,1024]{1,0:T(8,128)(2,1)} %gate_out_ref.1, bf16[3,128,128]{2,1,0:T(8,128)(2,1)} %analysis_hbm.1, bf16[3,128,128]{2,1,0:T(8,128)(2,1)} %synthesis_hbm.1, ...), custom_call_target="tpu_custom_call" | custom-call | tf_op jit(solution)/shard_map/pallas_call | solution.py:368
  81.8 2.1 %copy.12 = bf16[96,4096]{1,0:T(8,128)(2,1)} copy(bf16[96,4096]{1,0:T(8,128)(2,1)} %shard_map.100) | data formatting | bytes 1572864
